TPU v7x, 32 devices: a whole 2x2x4 slice. The times are simulated.
32 devices in a mesh: parts: 2 (over y), tensor: 4 (over z), dp: 4 (over x, core).
Axes of the slice: x: 2, y: 2, z: 4, core: 2. Of those that a mesh axis runs over, the one named last changes fastest.
Arguments:
- inputs: bfloat16 [3584, 8192], P(('parts', 'dp'), 'tensor'), parts along dimension 0, may hold values from -6 to 6
- out_grad: bfloat16 [3584, 8192], P(('parts', 'dp'), 'tensor'), parts along dimension 0, may hold values from -6 to 6
- gate_pre: bfloat16 [3584, 14784], P(('parts', 'dp'), 'tensor'), parts along dimension 0, may hold values from -5 to 5
- up_pre: bfloat16 [3584, 14784], P(('parts', 'dp'), 'tensor'), parts along dimension 0, may hold values from -5 to 5
- down_weight: bfloat16 [14784, 8192], P('tensor', 'dp'), may hold values from -0.0625 to 0.0625
- in_gate: bfloat16 [8192, 64], P('tensor'), may hold values from -0.0625 to 0.0625
- out_gate: bfloat16 [14784, 64], P('tensor'), may hold values from -0.046875 to 0.046875
- in_up: bfloat16 [8192, 64], P('tensor'), may hold values from -0.0625 to 0.0625
- out_up: bfloat16 [14784, 64], P('tensor'), may hold values from -0.046875 to 0.046875
- in_down: bfloat16 [14784, 64], P('tensor'), may hold values from -0.046875 to 0.046875
- out_down: bfloat16 [8192, 64], P('tensor'), may hold values from -0.0625 to 0.0625
- counts: int32 [16], P(('parts', 'dp')), parts along dimension 0, may hold values from 56 to 224, as said below
- query_ids: int32 [16], P('parts'), parts along dimension 0, may hold values from 0 to 7, as said below
Outputs:
- sketches: float32 [16, 3, 4096], P(('parts', 'dp')), parts along dimension 0
- scores: float32 [16, 8], P(('parts', 'dp')), parts along dimension 0
There are 2 independent parts, one for each index of `parts`. A program takes and returns all parts, laid end to end along the dimension named above; an argument that names none is the same for every part. Nothing has to cross between parts.
Inputs may be any that keep to these rules, and one draw needn't show every extreme that they name: The valid tokens are the first counts[e] slots of example e. `query_ids`: distinct example indices.
All inputs are finite; a program needn't handle non-finite values.
Results may differ from a plain program's by a relative error of at most 0.0029.
Values may be sent and summed in bfloat16 or wider, within the bound.
A program may use at most 256 MiB of HBM per device.

v0:
```python
import math

import jax
import jax.numpy as jnp
from jax import lax
from jax.sharding import PartitionSpec as P

SEQ = 224


def token_weights(rows, counts):
    slot = rows // SEQ
    place = rows % SEQ
    owners = jnp.arange(counts.shape[0], dtype=jnp.int32)
    hit = (slot[None, :] == owners[:, None]) & (place[None, :] < counts[:, None])
    return hit.astype(jnp.float32) * (1.0 / math.sqrt(SEQ))


def outer_sums(proj, weights):
    shaped = proj.reshape(proj.shape[0], 3, 2, -1)
    result = jnp.einsum(
        "en,nli,nlj->elij",
        weights,
        shaped[:, :, 0, :],
        shaped[:, :, 1, :],
        precision=lax.Precision.HIGHEST,
    )
    return result.reshape(result.shape[0], 3, -1)


def cosines(sketches, query):
    left = sketches.reshape(sketches.shape[0], -1)
    right = query.reshape(query.shape[0], -1)
    inner = jnp.einsum("ef,qf->eq", left, right, precision=lax.Precision.HIGHEST)
    left_norm = jnp.sqrt(jnp.sum(left * left, axis=1) + 1e-06)
    right_norm = jnp.sqrt(jnp.sum(right * right, axis=1) + 1e-06)
    return inner / (left_norm[:, None] * right_norm[None, :])


def contract_cols(left, right):
    return lax.dot_general(
        left, right, (((1,), (1,)), ((), ())), preferred_element_type=jnp.float32
    )


def shards(
    inputs,
    out_grad,
    gate_pre,
    up_pre,
    down_weight,
    in_gate,
    out_gate,
    in_up,
    out_up,
    in_down,
    out_down,
    counts,
    query_ids,
):
    tok_rows = inputs.shape[0]
    full_grad = lax.all_gather(out_grad, "tensor", axis=1, tiled=True)
    grad_hidden = contract_cols(full_grad, lax.all_gather(down_weight, "dp", axis=1, tiled=True))
    gate_value = gate_pre.astype(jnp.float32)
    up_value = up_pre.astype(jnp.float32)
    sigmoid_gate = jax.nn.sigmoid(gate_value)
    hidden = (gate_value * sigmoid_gate * up_value).astype(jnp.bfloat16)
    grad_up = (grad_hidden * gate_value * sigmoid_gate).astype(jnp.bfloat16)
    grad_gate = (
        grad_hidden * up_value * sigmoid_gate * (1.0 + gate_value * (1.0 - sigmoid_gate))
    ).astype(jnp.bfloat16)
    partial_proj = jnp.concatenate(
        [
            jnp.dot(inputs, in_gate, preferred_element_type=jnp.float32),
            jnp.dot(grad_gate, out_gate, preferred_element_type=jnp.float32),
            jnp.dot(inputs, in_up, preferred_element_type=jnp.float32),
            jnp.dot(grad_up, out_up, preferred_element_type=jnp.float32),
            jnp.dot(hidden, in_down, preferred_element_type=jnp.float32),
            jnp.dot(out_grad, out_down, preferred_element_type=jnp.float32),
        ],
        axis=1,
    )
    proj = lax.psum(partial_proj, "tensor")
    weights = token_weights(jnp.arange(tok_rows, dtype=jnp.int32), counts)
    sketches = outer_sums(proj, weights)
    every_sketch = lax.all_gather(sketches.astype(jnp.bfloat16), "dp", axis=0, tiled=True).astype(
        sketches.dtype
    )
    owners = jnp.arange(every_sketch.shape[0], dtype=jnp.int32)
    select = (query_ids[:, None] == owners[None, :]).astype(jnp.float32)
    query = jnp.einsum("qe,elf->qlf", select, every_sketch, precision=lax.Precision.HIGHEST)
    return (sketches, cosines(sketches, query))


def solution(mesh):
    return jax.shard_map(
        shards,
        mesh=mesh,
        in_specs=(
            P(("parts", "dp"), "tensor"),
            P(("parts", "dp"), "tensor"),
            P(("parts", "dp"), "tensor"),
            P(("parts", "dp"), "tensor"),
            P("tensor", "dp"),
            P("tensor", None),
            P("tensor", None),
            P("tensor", None),
            P("tensor", None),
            P("tensor", None),
            P("tensor", None),
            P(("parts", "dp")),
            P("parts"),
        ),
        out_specs=(P(("parts", "dp"), None, None), P(("parts", "dp"), None)),
        check_vma=False,
    )
```

profile of v0, /device:TPU:0, one launch (start us, length us, event | category | flops | bytes accessed | tf_op | source)
XLA Modules:
  0.0 613.4 jit_solution(7058288902857388005)
XLA Ops:
  7.2 0.0 copy-start
  7.2 0.0 all-gather.3.cloned.1.call-start
  7.2 0.7 all-gather.3.cloned.1.call-update
  7.9 0.0 copy-start.3
  7.9 0.0 all-gather.5.cloned.1.call-start
  8.0 0.7 all-gather.5.cloned.1.call-update
  8.7 0.0 all-reduce.2.cloned.1.call-start
  8.7 0.0 copy-done
  8.7 0.3 copy-done.3
  9.0 0.7 convolution_dynamic-update-slice_fusion.2
  9.7 0.0 copy-start.10
  9.7 135.1 %all-gather.3.cloned.1.call-done = bf16[448,8192]{1,0:T(8,128)(2,1)} async-done(((bf16[448,2048]{1,0:T(8,128)(2,1)}), bf16[448,8192]{1,0:T(8,128)(2,1)}) %all-gather.3.cloned.1.call-update) | async-done | bytes 7340048 | tf_op jit(solution)/shard_map/all_gather | solution.py:62
  144.8 355.9 %all-gather.5.cloned.1.call-done = bf16[3696,8192]{1,0:T(8,128)(2,1)} async-done(((bf16[3696,2048]{1,0:T(8,128)(2,1)}), bf16[3696,8192]{1,0:T(8,128)(2,1)}) %all-gather.5.cloned.1.call-update) | async-done | bytes 60555280 | tf_op jit(solution)/shard_map/all_gather | solution.py:63
  500.8 37.2 %fusion.44 = f32[448,3696]{1,0:T(8,128)} fusion(bf16[448,8192]{1,0:T(8,128)(2,1)} %all-gather.3.cloned.1.call-done, bf16[3696,8192]{1,0:T(8,128)(2,1)} %all-gather.5.cloned.1.call-done), kind=kOutput, calls=%fused_computation.57 | convolution fusion | flops 27128758272 | bytes 74518528 | tf_op jit(solution)/shard_map/dot_general | solution.py:41
  537.9 0.0 copy-done.10
  537.9 0.0 copy-start.4
  537.9 0.0 copy-start.9
  537.9 0.0 copy-start.11
  538.0 0.0 copy-start.13
  538.0 6.8 %fusion.16 = f32[448,384]{0,1:T(8,128)S(1)} fusion(f32[448,384]{0,1:T(8,128)S(1)} %convolution_dynamic-update-slice_fusion.2, bf16[3696,64]{0,1:T(8,128)(2,1)S(1)} %copy-done.10, f32[448,3696]{1,0:T(8,128)} %fusion.44, bf16[448,3696]{1,0:T(8,128)(2,1)} %param.16, bf16[448,3696]{1,0:T(8,128)(2,1)} %param.15), kind=kOutput, calls=%fused_computation.23 | convolution fusion | flops 231813120 | bytes 13852672 | tf_op jit(solution)/shard_map/dot_general | solution.py:75
  544.7 0.0 copy-done.4
  544.7 0.7 convolution_dynamic-update-slice_fusion.1
  545.4 0.0 copy-done.9
  545.4 0.0 copy-done.11
  545.4 0.5 copy-done.13
  545.9 0.0 copy-start.8
  545.9 0.0 copy-start.12
  545.9 1.9 fusion.19
  547.9 0.0 copy-done.8
  547.9 0.1 copy-done.12
  548.0 0.0 copy-start.1
  548.0 0.0 copy-start.5
  548.0 0.0 copy-start.7
  548.0 2.2 fusion.22
  550.2 0.0 copy-done.1
  550.2 0.0 copy-done.5
  550.2 0.0 copy-start.6
  550.2 0.6 convolution_dynamic-update-slice_fusion
  550.9 1.0 copy.22
  551.8 0.0 all-reduce.2.cloned.1.call-update
  551.9 0.0 copy-done.7
  551.9 0.1 fusion.30
  552.0 43.7 %all-reduce.2.cloned.1.call-done = f32[448,3,2,64]{0,3,1,2:T(8,128)} async-done(((f32[448,3,2,64]{0,3,1,2:T(8,128)}), f32[448,3,2,64]{0,3,1,2:T(8,128)}) %all-reduce.2.cloned.1.call-update) | async-done | bytes 688144 | tf_op jit(solution)/shard_map/psum | solution.py:83
  595.7 1.0 slice_bitcast_fusion.2
  596.7 1.9 multiply_reduce_fusion.1
  598.6 0.1 reshape.43
  598.8 0.0 copy-start.2
  598.8 0.1 reshape_reshape.3
  599.0 5.8 all_gather.11
  604.8 0.0 copy-done.6
  604.8 0.4 multiply_reduce_fusion
  605.3 1.6 convolution_divide_fusion
  606.9 0.0 copy-done.2
  (6 shorter events, 0.1 us)
Async XLA Ops:
  7.2 1.6 copy-start
  7.2 137.6 %all-gather.3.cloned.1.call-start = ((), (), s32[]{:S(2)}) async-start(), calls=%async_computation | async-start | bytes 9175040 | tf_op jit(solution)/shard_map/all_gather | solution.py:62
  7.9 1.1 copy-start.3
  7.9 492.8 %all-gather.5.cloned.1.call-start = ((), (), s32[]{:S(2)}) async-start(), calls=%async_computation.1 | async-start | bytes 75694080 | tf_op jit(solution)/shard_map/all_gather | solution.py:63
  8.7 587.0 %all-reduce.2.cloned.1.call-start = ((), (), s32[]{:S(2)}) async-start(), calls=%async_computation.2 | async-start | bytes 1572864 | tf_op jit(solution)/shard_map/psum | solution.py:83
  9.7 528.3 %copy-start.10 = (bf16[3696,64]{0,1:T(8,128)(2,1)S(1)}, bf16[3696,64]{0,1:T(8,128)(2,1)}, u32[]{:S(2)}) copy-start(bf16[3696,64]{0,1:T(8,128)(2,1)} %param.19) | copy-start | bytes 1419268
  537.9 6.8 %copy-start.4 = (bf16[2048,64]{0,1:T(8,128)(2,1)S(1)}, bf16[2048,64]{0,1:T(8,128)(2,1)}, u32[]{:S(2)}) copy-start(bf16[2048,64]{0,1:T(8,128)(2,1)} %param.20) | copy-start | bytes 786436
  537.9 7.5 %copy-start.9 = (bf16[448,3696]{1,0:T(8,128)(2,1)S(1)}, bf16[448,3696]{1,0:T(8,128)(2,1)}, u32[]{:S(2)}) copy-start(bf16[448,3696]{1,0:T(8,128)(2,1)} %param.15) | copy-start | bytes 9934852
  537.9 7.5 %copy-start.11 = (bf16[3696,64]{0,1:T(8,128)(2,1)S(1)}, bf16[3696,64]{0,1:T(8,128)(2,1)}, u32[]{:S(2)}) copy-start(bf16[3696,64]{0,1:T(8,128)(2,1)} %param.21) | copy-start | bytes 1419268
  538.0 8.0 %copy-start.13 = (f32[448,3696]{1,0:T(8,128)S(1)}, f32[448,3696]{1,0:T(8,128)}, u32[]{:S(2)}) copy-start(f32[448,3696]{1,0:T(8,128)} %fusion.44) | copy-start | bytes 19869700
  545.9 1.9 copy-start.8
  545.9 2.0 copy-start.12
  548.0 2.2 copy-start.1
  548.0 2.2 copy-start.5
  548.0 3.9 copy-start.7
  550.2 54.6 %copy-start.6 = (s32[8]{0:T(128)S(1)}, s32[8]{0:T(128)}, u32[]{:S(2)}) copy-start(s32[8]{0:T(128)} %param.25) | copy-start | bytes 100
  598.8 8.1 %copy-start.2 = (f32[2,3,4096]{2,0,1:T(2,128)}, f32[2,3,4096]{2,0,1:T(2,128)S(1)}, u32[]{:S(2)}) copy-start(f32[2,3,4096]{2,0,1:T(2,128)S(1)} %reshape.43) | copy-start | bytes 294916
Sparse Core Ops, SparseCore 0:
  9.6 135.1 all-gather.2
  146.4 354.3 all-gather.4
  552.0 43.6 all-reduce.1
where the time goes:
time: 614 us; the launch traced here: 613 us
  waiting for transfers between devices  536 us (87%)
  matrix products  54 us (9%)
  between operations  13.9 us (2%)
    all_gather x1, waiting for transfers between devices, shards(): lax.all_gather(down_weight, 'dp', axis=1, tiled=True)  356 us
    all_gather x1, waiting for transfers between devices, shards(): full_grad = lax.all_gather(out_grad, 'tensor', axis=1, tiled=True)  135 us
    psum x1, waiting for transfers between devices, shards(): proj = lax.psum(partial_proj, 'tensor')  43.7 us
    dot_general x1, matrix products, contract_cols(): lax.dot_general(left, right, (((1,), (1,)), ((), ())), preferred_element_...  37.2 us
  transfers between devices with their start and end apart: 3, of which 3 were waited for; matrix products, arithmetic and copies ran while one was open for 0% of the time, Pallas kernels for 0%

commit v1 on v0

--- a/solution.py
+++ b/solution.py
@@ -1,8 +1,11 @@
+import functools
 import math
 
 import jax
 import jax.numpy as jnp
 from jax import lax
+from jax.experimental import pallas as pl
+from jax.experimental.pallas import tpu as pltpu
 from jax.sharding import PartitionSpec as P
 
 SEQ = 224
@@ -43,7 +46,387 @@
     )
 
 
+CHUNK = 256
+AHEAD = 4
+PIECES = 4
+MESH = pl.DeviceIdType.MESH
+
+
+def backprop_kernel(
+    w_ref,
+    g_ref,
+    gate_ref,
+    up_ref,
+    og_ref,
+    ou_ref,
+    id_ref,
+    proj_ref,
+    wbuf,
+    gbuf,
+    gate_v,
+    up_v,
+    wv,
+    own_sem,
+    ld_sem,
+    x_send,
+    x_recv,
+    y_send,
+    y_recv,
+    s_send,
+    s_recv,
+    dn_send,
+    dn_recv,
+    up_send,
+    up_recv,
+):
+    hidden_rows, depth = w_ref.shape
+    tokens = g_ref.shape[0]
+    blocks = gbuf.shape[0]
+    half = depth // 2
+    full = hidden_rows // CHUNK
+    last = hidden_rows - full * CHUNK
+    piece = tokens // PIECES
+    z_steps = PIECES * (blocks - 1)
+
+    y = lax.axis_index("parts")
+    z = lax.axis_index("tensor")
+    d = lax.axis_index("dp")
+    sib = d + 1 - 2 * (d % 2)
+    far = (d + 2) % 4
+    far_sib = far + 1 - 2 * (far % 2)
+
+    def rows_of(k, rows):
+        return pl.ds(pl.multiple_of(k * CHUNK, CHUNK), rows)
+
+    def cols_of(h):
+        return pl.ds(pl.multiple_of(h * half, half), half)
+
+    def remote(src, dst, send, recv, device):
+        return pltpu.make_async_remote_copy(
+            src_ref=src,
+            dst_ref=dst,
+            send_sem=send,
+            recv_sem=recv,
+            device_id=device,
+            device_id_type=MESH,
+        )
+
+    def x_copy(k, rows):
+        r = rows_of(k, rows)
+        return remote(
+            w_ref.at[r, cols_of(y)],
+            wbuf.at[d, r, cols_of(y)],
+            x_send.at[k],
+            x_recv.at[k],
+            {"dp": far},
+        )
+
+    def x_arrival(k, rows):
+        r = rows_of(k, rows)
+        return remote(
+            w_ref.at[r, cols_of(y)],
+            wbuf.at[far, r, cols_of(y)],
+            x_send.at[k],
+            x_recv.at[k],
+            {"dp": far},
+        )
+
+    def y_copy(k, rows):
+        r = rows_of(k, rows)
+        block = wbuf.at[far, r, cols_of(y)]
+        return remote(block, block, y_send.at[k], y_recv.at[k], {"parts": 1 - y})
+
+    def y_arrival(k, rows):
+        r = rows_of(k, rows)
+        block = wbuf.at[far, r, cols_of(1 - y)]
+        return remote(block, block, y_send.at[k], y_recv.at[k], {"parts": 1 - y})
+
+    def s0_copy(k, rows, block):
+        r = rows_of(k, rows)
+        return remote(
+            w_ref.at[r], wbuf.at[block, r], s_send.at[0, k], s_recv.at[0, k], {"dp": sib}
+        )
+
+    def s_copy(kind, k, rows, block):
+        r = rows_of(k, rows)
+        h = y if kind == 1 else 1 - y
+        view = wbuf.at[block, r, cols_of(h)]
+        return remote(view, view, s_send.at[kind, k], s_recv.at[kind, k], {"dp": sib})
+
+    def z_rows(n):
+        return pl.ds(pl.multiple_of((n % PIECES) * piece, piece), piece)
+
+    def dn_copy(n, first):
+        view = gbuf.at[first + n // PIECES, z_rows(n)]
+        return remote(view, view, dn_send.at[n], dn_recv.at[n], {"tensor": z - 1})
+
+    def up_copy(n, first):
+        view = gbuf.at[first - n // PIECES, z_rows(n)]
+        return remote(view, view, up_send.at[n], up_recv.at[n], {"tensor": z + 1})
+
+    def z_duty(n):
+        @pl.when(n < PIECES * (blocks - 1 - z))
+        def _():
+            dn_copy(n, z + 1).wait_recv()
+
+            @pl.when(z > 0)
+            def _():
+                dn_copy(n + PIECES, z).start()
+
+        @pl.when(n < PIECES * z)
+        def _():
+            up_copy(n, z - 1).wait_recv()
+
+            @pl.when(z < blocks - 1)
+            def _():
+                up_copy(n + PIECES, z).start()
+
+    own_g = pltpu.make_async_copy(g_ref, gbuf.at[z], own_sem.at[0])
+    own_w = pltpu.make_async_copy(w_ref, wbuf.at[d], own_sem.at[1])
+    own_gate = pltpu.make_async_copy(gate_ref, gate_v, own_sem.at[2])
+    own_up = pltpu.make_async_copy(up_ref, up_v, own_sem.at[3])
+    own_g.start()
+
+    barrier = pltpu.get_barrier_semaphore()
+    for device in ({"dp": sib}, {"dp": far}, {"parts": 1 - y}):
+        pl.semaphore_signal(barrier, inc=1, device_id=device, device_id_type=MESH)
+
+    @pl.when(z > 0)
+    def _():
+        pl.semaphore_signal(barrier, inc=1, device_id={"tensor": z - 1}, device_id_type=MESH)
+
+    @pl.when(z < blocks - 1)
+    def _():
+        pl.semaphore_signal(barrier, inc=1, device_id={"tensor": z + 1}, device_id_type=MESH)
+
+    neighbours = 3 + (z > 0).astype(jnp.int32) + (z < blocks - 1).astype(jnp.int32)
+    pl.semaphore_wait(barrier, neighbours)
+
+    def open_chunk(k, rows):
+        x_copy(k, rows).start()
+        s0_copy(k, rows, d).start()
+
+    for k in range(AHEAD):
+        open_chunk(k, CHUNK)
+    own_g.wait()
+
+    @pl.when(z > 0)
+    def _():
+        for n in range(PIECES):
+            dn_copy(n, z).start()
+
+    @pl.when(z < blocks - 1)
+    def _():
+        for n in range(PIECES):
+            up_copy(n, z).start()
+
+    own_w.start()
+    own_gate.start()
+    own_up.start()
+    proj_ref[...] = jnp.zeros_like(proj_ref)
+
+    def take_x(k, rows):
+        x_arrival(k, rows).wait_recv()
+        y_copy(k, rows).start()
+        s_copy(1, k, rows, far).start()
+        s0_copy(k, rows, sib).wait_recv()
+
+    def take_y(k, rows):
+        y_arrival(k, rows).wait_recv()
+        s_copy(2, k, rows, far).start()
+        s_copy(1, k, rows, far_sib).wait_recv()
+
+    def take_s(k, rows):
+        s_copy(2, k, rows, far_sib).wait_recv()
+
+    def traffic(k):
+        take_x(k, CHUNK)
+
+        @pl.when(k >= 1)
+        def _():
+            take_y(k - 1, CHUNK)
+
+        @pl.when(k >= 2)
+        def _():
+            take_s(k - 2, CHUNK)
+
+        @pl.when(k + AHEAD < full)
+        def _():
+            open_chunk(k + AHEAD, CHUNK)
+
+        if last:
+
+            @pl.when(k + AHEAD == full)
+            def _():
+                open_chunk(full, last)
+
+    def loads(f, rows):
+        slot = f % 2
+        r = rows_of(f, rows)
+        return [
+            pltpu.make_async_copy(
+                wbuf.at[b, r], wv.at[slot, b, pl.ds(0, rows)], ld_sem.at[slot, b]
+            )
+            for b in range(blocks)
+        ]
+
+    def tile(f, rows, next_rows):
+        for copy in loads(f, rows):
+            copy.wait()
+        if next_rows:
+            for copy in loads(f + 1, next_rows):
+                copy.start()
+        slot = f % 2
+        r = rows_of(f, rows)
+        grad = None
+        for b in range(blocks):
+            term = lax.dot_general(
+                gbuf[b],
+                wv[slot, b, pl.ds(0, rows), :],
+                (((1,), (1,)), ((), ())),
+                preferred_element_type=jnp.float32,
+            )
+            grad = term if grad is None else grad + term
+        gate_value = gate_v[:, r].astype(jnp.float32)
+        up_value = up_v[:, r].astype(jnp.float32)
+        sig = 1.0 / (1.0 + jnp.exp(-gate_value))
+        hidden = (gate_value * sig * up_value).astype(jnp.bfloat16)
+        grad_up = (grad * gate_value * sig).astype(jnp.bfloat16)
+        grad_gate = (grad * up_value * sig * (1.0 + gate_value * (1.0 - sig))).astype(jnp.bfloat16)
+        proj_ref[0] += jnp.dot(grad_gate, og_ref[r, :], preferred_element_type=jnp.float32)
+        proj_ref[1] += jnp.dot(grad_up, ou_ref[r, :], preferred_element_type=jnp.float32)
+        proj_ref[2] += jnp.dot(hidden, id_ref[r, :], preferred_element_type=jnp.float32)
+
+    def tiles(lo, hi):
+        @pl.loop(lo, hi)
+        def _(f):
+            tile(f, CHUNK, CHUNK)
+
+    @pl.loop(0, z_steps)
+    def _(k):
+        z_duty(k)
+        traffic(k)
+
+    own_w.wait()
+    own_gate.wait()
+    own_up.wait()
+    for copy in loads(0, CHUNK):
+        copy.start()
+
+    done = 0
+    for k in range(z_steps, full):
+        traffic(k)
+        ready = k - 2
+        step = min(ready, done + 5)
+        tiles(done, step)
+        done = step
+    if last:
+        take_x(full, last)
+    take_y(full - 1, CHUNK)
+    take_s(full - 2, CHUNK)
+    tiles(done, full - 2)
+    if last:
+        take_y(full, last)
+    take_s(full - 1, CHUNK)
+    tiles(full - 2, full - 1)
+    if last:
+        take_s(full, last)
+    tile(full - 1, CHUNK, last)
+    if last:
+        tile(full, last, 0)
+
+    def drain(k, rows):
+        x_copy(k, rows).wait_send()
+        y_copy(k, rows).wait_send()
+        s0_copy(k, rows, d).wait_send()
+        s_copy(1, k, rows, far).wait_send()
+        s_copy(2, k, rows, far).wait_send()
+
+    @pl.loop(0, full)
+    def _(k):
+        drain(k, CHUNK)
+
+    if last:
+        drain(full, last)
+
+    @pl.loop(0, z_steps)
+    def _(n):
+        @pl.when((z > 0) & (n < PIECES * (blocks - z)))
+        def _():
+            dn_copy(n, z).wait_send()
+
+        @pl.when((z < blocks - 1) & (n < PIECES * (z + 1)))
+        def _():
+            up_copy(n, z).wait_send()
+
+
+def backprop(down_weight, out_grad, gate_pre, up_pre, out_gate, out_up, in_down, blocks):
+    hidden_rows, depth = down_weight.shape
+    tokens = out_grad.shape[0]
+    rank = out_gate.shape[1]
+    chunks = pl.cdiv(hidden_rows, CHUNK)
+    z_steps = PIECES * (blocks - 1)
+    anywhere = pl.BlockSpec(memory_space=pl.ANY)
+    local = pl.BlockSpec(memory_space=pltpu.VMEM)
+    dma = pltpu.SemaphoreType.DMA
+    proj, _ = pl.pallas_call(
+        backprop_kernel,
+        out_shape=(
+            jax.ShapeDtypeStruct((3, tokens, rank), jnp.float32),
+            jax.ShapeDtypeStruct((blocks, hidden_rows, depth), jnp.bfloat16),
+        ),
+        in_specs=[anywhere] * 4 + [local] * 3,
+        out_specs=(local, anywhere),
+        scratch_shapes=[
+            pltpu.VMEM((blocks, tokens, depth), jnp.bfloat16),
+            pltpu.VMEM(gate_pre.shape, jnp.bfloat16),
+            pltpu.VMEM(up_pre.shape, jnp.bfloat16),
+            pltpu.VMEM((2, blocks, CHUNK, depth), jnp.bfloat16),
+            dma((4,)),
+            dma((2, blocks)),
+            dma((chunks,)),
+            dma((chunks,)),
+            dma((chunks,)),
+            dma((chunks,)),
+            dma((3, chunks)),
+            dma((3, chunks)),
+            dma((z_steps,)),
+            dma((z_steps,)),
+            dma((z_steps,)),
+            dma((z_steps,)),
+        ],
+        compiler_params=pltpu.CompilerParams(
+            collective_id=0, has_side_effects=True, vmem_limit_bytes=50 * 2**20
+        ),
+        cost_estimate=pl.CostEstimate(
+            flops=2 * tokens * hidden_rows * depth * blocks,
+            bytes_accessed=2 * blocks * hidden_rows * depth * 2,
+            transcendentals=tokens * hidden_rows,
+        ),
+    )(down_weight, out_grad, gate_pre, up_pre, out_gate, out_up, in_down)
+    return proj
+
+
+def gathered(out_grad, gate_pre, up_pre, down_weight, out_gate, out_up, in_down):
+    full_grad = lax.all_gather(out_grad, "tensor", axis=1, tiled=True)
+    grad_hidden = contract_cols(full_grad, lax.all_gather(down_weight, "dp", axis=1, tiled=True))
+    gate_value = gate_pre.astype(jnp.float32)
+    up_value = up_pre.astype(jnp.float32)
+    sigmoid_gate = jax.nn.sigmoid(gate_value)
+    hidden = (gate_value * sigmoid_gate * up_value).astype(jnp.bfloat16)
+    grad_up = (grad_hidden * gate_value * sigmoid_gate).astype(jnp.bfloat16)
+    grad_gate = (
+        grad_hidden * up_value * sigmoid_gate * (1.0 + gate_value * (1.0 - sigmoid_gate))
+    ).astype(jnp.bfloat16)
+    return (
+        jnp.dot(grad_gate, out_gate, preferred_element_type=jnp.float32),
+        jnp.dot(grad_up, out_up, preferred_element_type=jnp.float32),
+        jnp.dot(hidden, in_down, preferred_element_type=jnp.float32),
+    )
+
+
 def shards(
+    fused,
     inputs,
     out_grad,
     gate_pre,
@@ -59,23 +442,19 @@
     query_ids,
 ):
     tok_rows = inputs.shape[0]
-    full_grad = lax.all_gather(out_grad, "tensor", axis=1, tiled=True)
-    grad_hidden = contract_cols(full_grad, lax.all_gather(down_weight, "dp", axis=1, tiled=True))
-    gate_value = gate_pre.astype(jnp.float32)
-    up_value = up_pre.astype(jnp.float32)
-    sigmoid_gate = jax.nn.sigmoid(gate_value)
-    hidden = (gate_value * sigmoid_gate * up_value).astype(jnp.bfloat16)
-    grad_up = (grad_hidden * gate_value * sigmoid_gate).astype(jnp.bfloat16)
-    grad_gate = (
-        grad_hidden * up_value * sigmoid_gate * (1.0 + gate_value * (1.0 - sigmoid_gate))
-    ).astype(jnp.bfloat16)
+    if fused:
+        grads = backprop(
+            down_weight, out_grad, gate_pre, up_pre, out_gate, out_up, in_down, lax.axis_size("tensor")
+        )
+    else:
+        grads = gathered(out_grad, gate_pre, up_pre, down_weight, out_gate, out_up, in_down)
     partial_proj = jnp.concatenate(
         [
             jnp.dot(inputs, in_gate, preferred_element_type=jnp.float32),
-            jnp.dot(grad_gate, out_gate, preferred_element_type=jnp.float32),
+            grads[0],
             jnp.dot(inputs, in_up, preferred_element_type=jnp.float32),
-            jnp.dot(grad_up, out_up, preferred_element_type=jnp.float32),
-            jnp.dot(hidden, in_down, preferred_element_type=jnp.float32),
+            grads[1],
+            grads[2],
             jnp.dot(out_grad, out_down, preferred_element_type=jnp.float32),
         ],
         axis=1,
@@ -93,8 +472,10 @@
 
 
 def solution(mesh):
+    sizes = dict(mesh.shape)
+    fused = sizes["parts"] == 2 and sizes["dp"] == 4 and sizes["tensor"] == 4
     return jax.shard_map(
-        shards,
+        functools.partial(shards, fused),
         mesh=mesh,
         in_specs=(
             P(("parts", "dp"), "tensor"),

time: 614 us -> 597 us (0.972)
  Pallas kernels: 0 us -> 514 us
  waiting for transfers between devices: 536 us -> 44 us
  matrix products: 54 us -> 5.82 us
  local copies, waits for them, and re-layouts: 3.23 us -> 12.8 us
    pallas_call x0 -> x1, Pallas kernels: none -> 514 us  [backprop(): pl.pallas_call(backprop_kernel, out_shape=(jax.ShapeDtypeStruct((3, token...]
    all_gather x2 -> x0, waiting for transfers between devices: 491 us -> none  [the longest x1 356 us: shards(): lax.all_gather(down_weight, 'dp', axis=1, tiled=True)]
    dot_general x4 -> x0, matrix products: 48.1 us -> none  [the longest x1 37.2 us: contract_cols(): lax.dot_general(left, right, (((1,), (1,)), ((), ())), preferred_element_...]
    unnamed x28 -> x25, local copies, waits for them, and re-layouts: 0.92 us -> 7.95 us
  transfers between devices with their start and end apart: 3 -> 1, of which waited for: 3 -> 1; matrix products, arithmetic and copies ran while one was open for 0% -> 0% of each run, Pallas kernels for 0% -> 0%
where the time goes in v1:
time: 597 us
  Pallas kernels  514 us (86%)
  waiting for transfers between devices  44 us (7%)
  between operations  14.2 us (2%)
  local copies, waits for them, and re-layouts  12.8 us (2%)
    pallas_call x1, Pallas kernels, backprop(): pl.pallas_call(backprop_kernel, out_shape=(jax.ShapeDtypeStruct((3, token...  514 us
    psum x1, waiting for transfers between devices, shards(): proj = lax.psum(partial_proj, 'tensor')  44 us
  transfers between devices with their start and end apart: 1, of which 1 were waited for; matrix products, arithmetic and copies ran while one was open for 0% of the time, Pallas kernels for 0%

profile of v1, /device:TPU:0, one launch (start us, length us, event | category | flops | bytes accessed | tf_op | source)
XLA Modules:
  0.0 596.6 jit_solution(15787649095859808930)
XLA Ops:
  7.2 0.0 copy-start
  7.2 0.0 copy-start.4
  7.2 0.0 all-reduce.2.cloned.1.call-start
  7.2 1.6 copy.42.og_ref
  8.9 2.3 copy.43.ou_ref
  11.2 0.0 copy-done.4
  11.2 1.3 copy.44.id_ref
  12.5 0.0 copy-start.1
  12.5 1.2 copy-done.1
  13.7 0.0 copy-start.2
  13.7 1.2 copy-done.2
  14.9 0.0 copy-start.6
  14.9 513.8 %shard_map.140 = (f32[3,448,64]{2,1,0:T(8,128)S(1)}, bf16[4,3696,2048]{2,1,0:T(8,128)(2,1)}) custom-call(bf16[3696,2048]{1,0:T(8,128)(2,1)} %w_ref.1, bf16[448,2048]{1,0:T(8,128)(2,1)} %g_ref.1, bf16[448,3696]{1,0:T(8,128)(2,1)} %gate_ref.1, bf16[448,3696]{1,0:T(8,128)(2,1)} %up_ref.1, bf16[3696,64]{1,0:T(8,128)(2,1)S(1)} %copy.42.og_ref, ...), custom_call_target="tpu_custom_call" | custom-call | flops 27128758272 | bytes 121110528 | tf_op jit(solution)/shard_map/pallas_call | solution.py:372
  528.8 0.0 copy-start.7
  528.8 0.8 slice_bitcast_fusion.3
  529.6 0.0 copy-done
  529.6 0.0 copy-done.6
  529.6 0.0 copy-start.3
  529.6 0.0 copy-start.8
  529.6 0.6 fusion.16
  530.2 0.0 copy-done.7
  530.2 0.6 fusion.17
  530.9 0.2 copy-done.3
  531.1 0.0 copy-done.8
  531.1 0.6 fusion.18
  531.7 1.4 concatenate.3
  533.2 0.0 copy-start.10
  533.2 0.3 copy.48
  533.4 1.0 copy.49
  534.4 0.0 copy-start.9
  534.4 0.0 all-reduce.2.cloned.1.call-update
  534.5 0.0 copy-done.10
  534.5 0.1 fusion.5
  534.5 44.0 %all-reduce.2.cloned.1.call-done = f32[448,3,2,64]{0,3,1,2:T(8,128)} async-done(((f32[448,3,2,64]{0,3,1,2:T(8,128)}), f32[448,3,2,64]{0,3,1,2:T(8,128)}) %all-reduce.2.cloned.1.call-update) | async-done | bytes 688144 | tf_op jit(solution)/shard_map/psum | solution.py:462
  578.5 1.0 slice_bitcast_fusion.2
  579.6 1.9 multiply_reduce_fusion.1
  581.5 0.1 reshape.43
  581.6 0.0 copy-start.5
  581.7 5.8 all_gather.3
  587.5 0.0 copy-done.9
  587.5 0.4 multiply_reduce_fusion
  588.0 0.1 reshape_reshape.3
  588.1 1.6 convolution_divide_fusion
  589.7 0.0 copy-done.5
  (6 shorter events, 0.1 us)
Async XLA Ops:
  7.2 522.4 %copy-start = (bf16[448,2048]{1,0:T(8,128)(2,1)S(1)}, bf16[448,2048]{1,0:T(8,128)(2,1)}, u32[]{:S(2)}) copy-start(bf16[448,2048]{1,0:T(8,128)(2,1)} %param.13) | copy-start | bytes 5505028
  7.2 4.0 copy-start.4
  7.2 571.3 %all-reduce.2.cloned.1.call-start = ((), (), s32[]{:S(2)}) async-start(), calls=%async_computation | async-start | bytes 1572864 | tf_op jit(solution)/shard_map/psum | solution.py:462
  12.5 1.2 copy-start.1
  13.7 1.2 copy-start.2
  14.9 514.7 %copy-start.6 = (bf16[2048,64]{0,1:T(8,128)(2,1)S(1)}, bf16[2048,64]{0,1:T(8,128)(2,1)}, u32[]{:S(2)}) copy-start(bf16[2048,64]{0,1:T(8,128)(2,1)} %param.18) | copy-start | bytes 786436
  528.8 1.5 copy-start.7
  529.6 1.5 copy-start.3
  529.6 1.5 copy-start.8
  533.2 1.3 copy-start.10
  534.4 53.1 %copy-start.9 = (s32[8]{0:T(128)S(1)}, s32[8]{0:T(128)}, u32[]{:S(2)}) copy-start(s32[8]{0:T(128)} %param.25) | copy-start | bytes 100
  581.6 8.1 %copy-start.5 = (f32[2,3,4096]{2,0,1:T(2,128)}, f32[2,3,4096]{2,0,1:T(2,128)S(1)}, u32[]{:S(2)}) copy-start(f32[2,3,4096]{2,0,1:T(2,128)S(1)} %reshape.43) | copy-start | bytes 294916
Sparse Core Ops, SparseCore 0:
  534.6 43.9 all-reduce.1

commit v2 on v1

--- a/solution.py
+++ b/solution.py
@@ -94,6 +94,7 @@
     sib = d + 1 - 2 * (d % 2)
     far = (d + 2) % 4
     far_sib = far + 1 - 2 * (far % 2)
+    order = (d, sib, far, far_sib)
 
     def rows_of(k, rows):
         return pl.ds(pl.multiple_of(k * CHUNK, CHUNK), rows)
@@ -182,9 +183,8 @@
                 up_copy(n + PIECES, z).start()
 
     own_g = pltpu.make_async_copy(g_ref, gbuf.at[z], own_sem.at[0])
-    own_w = pltpu.make_async_copy(w_ref, wbuf.at[d], own_sem.at[1])
-    own_gate = pltpu.make_async_copy(gate_ref, gate_v, own_sem.at[2])
-    own_up = pltpu.make_async_copy(up_ref, up_v, own_sem.at[3])
+    own_gate = pltpu.make_async_copy(gate_ref, gate_v, own_sem.at[1])
+    own_up = pltpu.make_async_copy(up_ref, up_v, own_sem.at[2])
     own_g.start()
 
     barrier = pltpu.get_barrier_semaphore()
@@ -220,7 +220,6 @@
         for n in range(PIECES):
             up_copy(n, z).start()
 
-    own_w.start()
     own_gate.start()
     own_up.start()
     proj_ref[...] = jnp.zeros_like(proj_ref)
@@ -263,11 +262,10 @@
     def loads(f, rows):
         slot = f % 2
         r = rows_of(f, rows)
+        sources = [w_ref.at[r]] + [wbuf.at[b, r] for b in order[1:]]
         return [
-            pltpu.make_async_copy(
-                wbuf.at[b, r], wv.at[slot, b, pl.ds(0, rows)], ld_sem.at[slot, b]
-            )
-            for b in range(blocks)
+            pltpu.make_async_copy(src, wv.at[slot, j, pl.ds(0, rows)], ld_sem.at[slot, j])
+            for j, src in enumerate(sources)
         ]
 
     def tile(f, rows, next_rows):
@@ -279,10 +277,10 @@
         slot = f % 2
         r = rows_of(f, rows)
         grad = None
-        for b in range(blocks):
+        for j, b in enumerate(order):
             term = lax.dot_general(
                 gbuf[b],
-                wv[slot, b, pl.ds(0, rows), :],
+                wv[slot, j, pl.ds(0, rows), :],
                 (((1,), (1,)), ((), ())),
                 preferred_element_type=jnp.float32,
             )
@@ -307,7 +305,6 @@
         z_duty(k)
         traffic(k)
 
-    own_w.wait()
     own_gate.wait()
     own_up.wait()
     for copy in loads(0, CHUNK):
@@ -382,7 +379,7 @@
             pltpu.VMEM(gate_pre.shape, jnp.bfloat16),
             pltpu.VMEM(up_pre.shape, jnp.bfloat16),
             pltpu.VMEM((2, blocks, CHUNK, depth), jnp.bfloat16),
-            dma((4,)),
+            dma((3,)),
             dma((2, blocks)),
             dma((chunks,)),
             dma((chunks,)),

time: 597 us -> 283 us (0.47)
  Pallas kernels: 514 us -> 200 us
    pallas_call x1, Pallas kernels: 514 us -> 200 us  [backprop(): pl.pallas_call(backprop_kernel, out_shape=(jax.ShapeDtypeStruct((3, token...]
where the time goes in v2:
time: 283 us; the launch traced here: 282 us
  Pallas kernels  200 us (71%)
  waiting for transfers between devices  43.4 us (15%)
  between operations  14.2 us (5%)
  local copies, waits for them, and re-layouts  12.8 us (5%)
  matrix products  5.82 us (2%)
  blocking collectives  5.79 us (2%)
    pallas_call x1, Pallas kernels, backprop(): pl.pallas_call(backprop_kernel, out_shape=(jax.ShapeDtypeStruct((3, token...  200 us
    psum x1, waiting for transfers between devices, shards(): proj = lax.psum(partial_proj, 'tensor')  43.4 us
    unnamed x25, local copies, waits for them, and re-layouts  7.95 us
    all_gather x1, blocking collectives, shards(): lax.all_gather(sketches.astype(jnp.bfloat16), 'dp', axis=0, tiled=True)  5.79 us
  transfers between devices with their start and end apart: 1, of which 1 were waited for; matrix products, arithmetic and copies ran while one was open for 0% of the time, Pallas kernels for 0%

profile of v2, /device:TPU:0, one launch (start us, length us, event | category | flops | bytes accessed | tf_op | source)
XLA Modules:
  0.0 282.3 jit_solution(10538938244660725271)
XLA Ops:
  7.2 0.0 copy-start
  7.2 0.0 copy-start.4
  7.2 0.0 all-reduce.2.cloned.1.call-start
  7.2 1.6 copy.42.og_ref
  8.9 2.3 copy.43.ou_ref
  11.2 0.0 copy-done.4
  11.2 1.3 copy.44.id_ref
  12.5 0.0 copy-start.1
  12.5 1.2 copy-done.1
  13.7 0.0 copy-start.2
  13.7 1.2 copy-done.2
  14.9 0.0 copy-start.6
  14.9 200.1 %shard_map.140 = (f32[3,448,64]{2,1,0:T(8,128)S(1)}, bf16[4,3696,2048]{2,1,0:T(8,128)(2,1)}) custom-call(bf16[3696,2048]{1,0:T(8,128)(2,1)} %w_ref.1, bf16[448,2048]{1,0:T(8,128)(2,1)} %g_ref.1, bf16[448,3696]{1,0:T(8,128)(2,1)} %gate_ref.1, bf16[448,3696]{1,0:T(8,128)(2,1)} %up_ref.1, bf16[3696,64]{1,0:T(8,128)(2,1)S(1)} %copy.42.og_ref, ...), custom_call_target="tpu_custom_call" | custom-call | flops 27128758272 | bytes 121110528 | tf_op jit(solution)/shard_map/pallas_call | solution.py:369
  215.0 0.0 copy-start.7
  215.0 0.8 slice_bitcast_fusion.3
  215.9 0.0 copy-done
  215.9 0.0 copy-done.6
  215.9 0.0 copy-start.3
  215.9 0.0 copy-start.8
  215.9 0.6 fusion.16
  216.5 0.0 copy-done.7
  216.5 0.6 fusion.17
  217.1 0.2 copy-done.3
  217.4 0.0 copy-done.8
  217.4 0.6 fusion.18
  218.0 1.4 concatenate.3
  219.4 0.0 copy-start.10
  219.4 0.3 copy.48
  219.7 1.0 copy.49
  220.7 0.0 copy-start.9
  220.7 0.0 all-reduce.2.cloned.1.call-update
  220.7 0.0 copy-done.10
  220.7 0.1 fusion.5
  220.8 43.4 %all-reduce.2.cloned.1.call-done = f32[448,3,2,64]{0,3,1,2:T(8,128)} async-done(((f32[448,3,2,64]{0,3,1,2:T(8,128)}), f32[448,3,2,64]{0,3,1,2:T(8,128)}) %all-reduce.2.cloned.1.call-update) | async-done | bytes 688144 | tf_op jit(solution)/shard_map/psum | solution.py:459
  264.2 1.0 slice_bitcast_fusion.2
  265.2 1.9 multiply_reduce_fusion.1
  267.2 0.1 reshape.43
  267.3 0.0 copy-start.5
  267.4 5.8 %all_gather.3 = bf16[8,3,4096]{2,1,0:T(4,128)(2,1)S(1)} all-gather(bf16[2,3,4096]{2,1,0:T(4,128)(2,1)S(1)} %copy.51), channel_id=1, replica_groups=mesh['parts'=2,'tensor'=4,'dp'=4] {'dp'}, dimensions={0}, use_global_device_ids=true | all-gather | bytes 245760 | tf_op jit(solution)/shard_map/all_gather | solution.py:462
  273.2 0.0 copy-done.9
  273.2 0.4 multiply_reduce_fusion
  273.7 0.1 reshape_reshape.3
  273.8 1.6 convolution_divide_fusion
  275.4 0.0 copy-done.5
  (6 shorter events, 0.1 us)
Async XLA Ops:
  7.2 208.7 %copy-start = (bf16[448,2048]{1,0:T(8,128)(2,1)S(1)}, bf16[448,2048]{1,0:T(8,128)(2,1)}, u32[]{:S(2)}) copy-start(bf16[448,2048]{1,0:T(8,128)(2,1)} %param.13) | copy-start | bytes 5505028
  7.2 4.0 %copy-start.4 = (bf16[3696,64]{0,1:T(8,128)(2,1)S(1)}, bf16[3696,64]{0,1:T(8,128)(2,1)}, u32[]{:S(2)}) copy-start(bf16[3696,64]{0,1:T(8,128)(2,1)} %param.22) | copy-start | bytes 1419268
  7.2 257.0 %all-reduce.2.cloned.1.call-start = ((), (), s32[]{:S(2)}) async-start(), calls=%async_computation | async-start | bytes 1572864 | tf_op jit(solution)/shard_map/psum | solution.py:459
  12.5 1.2 copy-start.1
  13.7 1.2 copy-start.2
  14.9 200.9 %copy-start.6 = (bf16[2048,64]{0,1:T(8,128)(2,1)S(1)}, bf16[2048,64]{0,1:T(8,128)(2,1)}, u32[]{:S(2)}) copy-start(bf16[2048,64]{0,1:T(8,128)(2,1)} %param.18) | copy-start | bytes 786436
  215.0 1.5 copy-start.7
  215.9 1.5 copy-start.3
  215.9 1.5 copy-start.8
  219.4 1.3 copy-start.10
  220.7 52.5 %copy-start.9 = (s32[8]{0:T(128)S(1)}, s32[8]{0:T(128)}, u32[]{:S(2)}) copy-start(s32[8]{0:T(128)} %param.25) | copy-start | bytes 100
  267.3 8.1 %copy-start.5 = (f32[2,3,4096]{2,0,1:T(2,128)}, f32[2,3,4096]{2,0,1:T(2,128)S(1)}, u32[]{:S(2)}) copy-start(f32[2,3,4096]{2,0,1:T(2,128)S(1)} %reshape.43) | copy-start | bytes 294916
Sparse Core Ops, SparseCore 0:
  220.8 43.3 all-reduce.1

commit v3 on v2

--- a/solution.py
+++ b/solution.py
@@ -291,9 +291,9 @@
         hidden = (gate_value * sig * up_value).astype(jnp.bfloat16)
         grad_up = (grad * gate_value * sig).astype(jnp.bfloat16)
         grad_gate = (grad * up_value * sig * (1.0 + gate_value * (1.0 - sig))).astype(jnp.bfloat16)
-        proj_ref[0] += jnp.dot(grad_gate, og_ref[r, :], preferred_element_type=jnp.float32)
-        proj_ref[1] += jnp.dot(grad_up, ou_ref[r, :], preferred_element_type=jnp.float32)
-        proj_ref[2] += jnp.dot(hidden, id_ref[r, :], preferred_element_type=jnp.float32)
+        proj_ref[0] += contract_cols(grad_gate, og_ref[:, r])
+        proj_ref[1] += contract_cols(grad_up, ou_ref[:, r])
+        proj_ref[2] += contract_cols(hidden, id_ref[:, r])
 
     def tiles(lo, hi):
         @pl.loop(lo, hi)
@@ -310,11 +310,12 @@
     for copy in loads(0, CHUNK):
         copy.start()
 
-    done = 0
+    done = 3
+    tiles(0, done)
     for k in range(z_steps, full):
         traffic(k)
         ready = k - 2
-        step = min(ready, done + 5)
+        step = min(ready, done + 4)
         tiles(done, step)
         done = step
     if last:
@@ -400,8 +401,110 @@
             bytes_accessed=2 * blocks * hidden_rows * depth * 2,
             transcendentals=tokens * hidden_rows,
         ),
-    )(down_weight, out_grad, gate_pre, up_pre, out_gate, out_up, in_down)
+    )(down_weight, out_grad, gate_pre, up_pre, out_gate.T, out_up.T, in_down.T)
     return proj
+
+
+def sketch_kernel(proj_ref, weight_ref, out_ref, rows_buf, sketch_buf, r_send, r_recv, k_send, k_recv):
+    parts = rows_buf.shape[0]
+    share = rows_buf.shape[1]
+    rank = sketch_buf.shape[2]
+    z = lax.axis_index("tensor")
+    barrier = pltpu.get_barrier_semaphore()
+    peers = [lax.rem(z + step, parts) for step in range(1, parts)]
+    for peer in peers:
+        pl.semaphore_signal(barrier, inc=1, device_id={"tensor": peer}, device_id_type=MESH)
+    pl.semaphore_wait(barrier, parts - 1)
+
+    def share_of(owner):
+        return pl.ds(pl.multiple_of(owner * share, share), share)
+
+    def rows_copy(i):
+        return pltpu.make_async_remote_copy(
+            src_ref=proj_ref.at[share_of(peers[i])],
+            dst_ref=rows_buf.at[z],
+            send_sem=r_send.at[i],
+            recv_sem=r_recv.at[i],
+            device_id={"tensor": peers[i]},
+            device_id_type=MESH,
+        )
+
+    def sketch_copy(i):
+        return pltpu.make_async_remote_copy(
+            src_ref=sketch_buf.at[z],
+            dst_ref=sketch_buf.at[z],
+            send_sem=k_send.at[i],
+            recv_sem=k_recv.at[i],
+            device_id={"tensor": peers[i]},
+            device_id_type=MESH,
+        )
+
+    for i in range(parts - 1):
+        rows_copy(i).start()
+    rows_buf[z] = proj_ref[share_of(z), :]
+    for i in range(parts - 1):
+        rows_copy(i).wait()
+    total = rows_buf[0]
+    for i in range(1, parts):
+        total = total + rows_buf[i]
+    scaled = total * weight_ref[share_of(z), :]
+    width = 2 * rank
+    products = []
+    for layer in range(3):
+        cols = slice(layer * width, (layer + 1) * width)
+        products.append(
+            lax.dot_general(
+                scaled[:, cols],
+                total[:, cols],
+                (((0,), (0,)), ((), ())),
+                precision=lax.Precision.HIGHEST,
+                preferred_element_type=jnp.float32,
+            )
+        )
+    lane = lax.broadcasted_iota(jnp.int32, (rank, width), 1)
+    sketch_buf[z, 0] = jnp.where(
+        lane < rank, products[1][rank:, :], products[0][:rank, :]
+    )
+    sketch_buf[z, 1] = products[2][:rank, :]
+    for i in range(parts - 1):
+        sketch_copy(i).start()
+    for i in range(parts - 1):
+        sketch_copy(i).wait()
+    examples = out_ref.shape[0]
+    each = parts // examples
+    for e in range(examples):
+        result = sketch_buf[e * each]
+        for i in range(1, each):
+            result = result + sketch_buf[e * each + i]
+        out_ref[e] = result
+
+
+def sketch_sums(proj, weights, parts):
+    tokens, width = proj.shape
+    examples = weights.shape[0]
+    rank = width // 6
+    share = tokens // parts
+    local = pl.BlockSpec(memory_space=pltpu.VMEM)
+    dma = pltpu.SemaphoreType.DMA
+    packed = pl.pallas_call(
+        sketch_kernel,
+        out_shape=jax.ShapeDtypeStruct((examples, 2, rank, 2 * rank), jnp.float32),
+        in_specs=[local, local],
+        out_specs=local,
+        scratch_shapes=[
+            pltpu.VMEM((parts, share, width), jnp.float32),
+            pltpu.VMEM((parts, 2, rank, 2 * rank), jnp.float32),
+            dma((parts - 1,)),
+            dma((parts - 1,)),
+            dma((parts - 1,)),
+            dma((parts - 1,)),
+        ],
+        compiler_params=pltpu.CompilerParams(
+            collective_id=1, has_side_effects=True, vmem_limit_bytes=24 * 2**20
+        ),
+    )(proj, jnp.sum(weights, axis=0)[:, None])
+    layers = [packed[:, 0, :, rank:], packed[:, 0, :, :rank], packed[:, 1, :, rank:]]
+    return jnp.stack(layers, axis=1).reshape(examples, 3, rank * rank)
 
 
 def gathered(out_grad, gate_pre, up_pre, down_weight, out_gate, out_up, in_down):
@@ -445,20 +548,19 @@
         )
     else:
         grads = gathered(out_grad, gate_pre, up_pre, down_weight, out_gate, out_up, in_down)
-    partial_proj = jnp.concatenate(
-        [
-            jnp.dot(inputs, in_gate, preferred_element_type=jnp.float32),
-            grads[0],
-            jnp.dot(inputs, in_up, preferred_element_type=jnp.float32),
-            grads[1],
-            grads[2],
-            jnp.dot(out_grad, out_down, preferred_element_type=jnp.float32),
-        ],
-        axis=1,
-    )
-    proj = lax.psum(partial_proj, "tensor")
+    in_proj = [
+        jnp.dot(inputs, in_gate, preferred_element_type=jnp.float32),
+        jnp.dot(inputs, in_up, preferred_element_type=jnp.float32),
+        jnp.dot(out_grad, out_down, preferred_element_type=jnp.float32),
+    ]
     weights = token_weights(jnp.arange(tok_rows, dtype=jnp.int32), counts)
-    sketches = outer_sums(proj, weights)
+    if fused:
+        columns = [in_proj[0], grads[0], grads[1], in_proj[1], grads[2], in_proj[2]]
+        sketches = sketch_sums(jnp.concatenate(columns, axis=1), weights, lax.axis_size("tensor"))
+    else:
+        columns = [in_proj[0], grads[0], in_proj[1], grads[1], grads[2], in_proj[2]]
+        proj = lax.psum(jnp.concatenate(columns, axis=1), "tensor")
+        sketches = outer_sums(proj, weights)
     every_sketch = lax.all_gather(sketches.astype(jnp.bfloat16), "dp", axis=0, tiled=True).astype(
         sketches.dtype
     )

time: 283 us -> 238 us (0.84)
  waiting for transfers between devices: 43.4 us -> 0 us
  Pallas kernels: 200 us -> 219 us
  between operations: 14.2 us -> 0.79 us
  local copies, waits for them, and re-layouts: 12.8 us -> 7.48 us
    psum x1 -> x0, waiting for transfers between devices: 43.4 us -> none  [shards(): proj = lax.psum(partial_proj, 'tensor')]
    pallas_call x0 -> x1, Pallas kernels: none -> 22.6 us  [sketch_sums(): pl.pallas_call(sketch_kernel, out_shape=jax.ShapeDtypeStruct((examples, 2...]
    pallas_call x1, Pallas kernels: 200 us -> 196 us  [backprop(): pl.pallas_call(backprop_kernel, out_shape=(jax.ShapeDtypeStruct((3, token...]
    unnamed x25 -> x20, local copies, waits for them, and re-layouts: 7.95 us -> 4.73 us
  transfers between devices with their start and end apart: 1 -> 0, of which waited for: 1 -> 0; matrix products, arithmetic and copies ran while one was open for 0% -> 0% of each run, Pallas kernels for 0% -> 0%
where the time goes in v3:
time: 238 us
  Pallas kernels  219 us (92%)
  local copies, waits for them, and re-layouts  7.48 us (3%)
  blocking collectives  5.79 us (2%)
  matrix products  3.89 us (2%)
    pallas_call x1, Pallas kernels, backprop(): pl.pallas_call(backprop_kernel, out_shape=(jax.ShapeDtypeStruct((3, token...  196 us
    pallas_call x1, Pallas kernels, sketch_sums(): pl.pallas_call(sketch_kernel, out_shape=jax.ShapeDtypeStruct((examples, 2...  22.6 us
    all_gather x1, blocking collectives, shards(): lax.all_gather(sketches.astype(jnp.bfloat16), 'dp', axis=0, tiled=True)  5.79 us

profile of v3, /device:TPU:0, one launch (start us, length us, event | category | flops | bytes accessed | tf_op | source)
XLA Modules:
  0.0 237.9 jit_solution(4705792675718835984)
XLA Ops:
  0.6 0.0 copy-start
  0.6 0.0 copy-start.1
  0.7 1.6 copy-done.1
  2.3 0.0 copy-start.2
  2.3 1.0 copy-done.2
  3.3 0.0 copy-start.3
  3.3 1.0 copy-done.3
  4.3 0.0 copy-start.4
  4.3 1.0 copy-done.4
  5.4 0.0 copy-start.5
  5.4 196.3 %shard_map.140 = (f32[3,448,64]{2,1,0:T(8,128)S(1)}, bf16[4,3696,2048]{2,1,0:T(8,128)(2,1)}) custom-call(bf16[3696,2048]{1,0:T(8,128)(2,1)} %w_ref.1, bf16[448,2048]{1,0:T(8,128)(2,1)S(1)} %copy-done.1, bf16[448,3696]{1,0:T(8,128)(2,1)} %gate_ref.1, bf16[448,3696]{1,0:T(8,128)(2,1)} %up_ref.1, bf16[64,3696]{1,0:T(8,128)(2,1)S(1)} %bitcast.28, ...), custom_call_target="tpu_custom_call" | custom-call | flops 27128758272 | bytes 121110528 | tf_op jit(solution)/shard_map/pallas_call | solution.py:370
  201.7 0.0 copy-start.6
  201.7 0.8 slice_bitcast_fusion
  202.5 0.0 copy-done
  202.5 0.0 copy-done.5
  202.5 0.0 copy-start.7
  202.5 0.6 fusion.15
  203.2 0.0 copy-done.6
  203.2 0.6 fusion.16
  203.8 0.0 copy-done.7
  203.8 0.0 copy-start.9
  203.8 0.6 fusion.17
  204.5 1.4 concatenate.3.proj_ref
  205.9 0.0 copy-start.8
  205.9 0.0 copy-done.9
  205.9 0.1 fusion.2
  206.0 0.1 copy.35.weight_ref
  206.1 22.6 %shard_map.141 = f32[2,2,64,128]{3,2,1,0:T(8,128)S(1)} custom-call(f32[448,384]{1,0:T(8,128)S(1)} %concatenate.3.proj_ref, f32[448,1]{1,0:T(8,128)S(1)} %copy.35.weight_ref), custom_call_target="tpu_custom_call" | custom-call | tf_op jit(solution)/shard_map/pallas_call | solution.py:489
  228.8 0.1 fusion.14
  228.9 0.1 multiply_reduce_fusion.1
  229.0 0.1 reshape.42
  229.1 0.7 fusion.13
  229.9 5.8 %all_gather.3 = bf16[8,3,4096]{2,1,0:T(4,128)(2,1)S(1)} all-gather(bf16[2,3,4096]{2,1,0:T(4,128)(2,1)S(1)} %copy.37), channel_id=1, replica_groups=mesh['parts'=2,'tensor'=4,'dp'=4] {'dp'}, dimensions={0}, use_global_device_ids=true | all-gather | bytes 245760 | tf_op jit(solution)/shard_map/all_gather | solution.py:564
  235.7 0.0 copy-done.8
  235.7 0.4 multiply_reduce_fusion
  236.2 0.1 reshape_reshape.3
  236.3 1.6 convolution_divide_fusion
  (4 shorter events, 0.1 us)
Async XLA Ops:
  0.6 201.9 %copy-start = (bf16[448,2048]{1,0:T(8,128)(2,1)S(1)}, bf16[448,2048]{1,0:T(8,128)(2,1)}, u32[]{:S(2)}) copy-start(bf16[448,2048]{1,0:T(8,128)(2,1)} %param.13) | copy-start | bytes 5505028
  0.6 1.6 copy-start.1
  2.3 1.0 copy-start.2
  3.3 1.0 copy-start.3
  4.3 1.0 copy-start.4
  5.4 197.2 %copy-start.5 = (bf16[2048,64]{0,1:T(8,128)(2,1)S(1)}, bf16[2048,64]{0,1:T(8,128)(2,1)}, u32[]{:S(2)}) copy-start(bf16[2048,64]{0,1:T(8,128)(2,1)} %param.18) | copy-start | bytes 786436
  201.7 1.5 copy-start.6
  202.5 1.3 copy-start.7
  203.8 2.1 copy-start.9
  205.9 29.9 %copy-start.8 = (s32[8]{0:T(128)S(1)}, s32[8]{0:T(128)}, u32[]{:S(2)}) copy-start(s32[8]{0:T(128)} %param.25) | copy-start | bytes 100

commit v4 on v3

--- a/solution.py
+++ b/solution.py
@@ -310,7 +310,7 @@
     for copy in loads(0, CHUNK):
         copy.start()
 
-    done = 3
+    done = 4
     tiles(0, done)
     for k in range(z_steps, full):
         traffic(k)

time: 238 us -> 242 us (1.017)
  Pallas kernels: 219 us -> 223 us
    pallas_call x1, Pallas kernels: 196 us -> 200 us  [backprop(): pl.pallas_call(backprop_kernel, out_shape=(jax.ShapeDtypeStruct((3, token...]
where the time goes in v4:
time: 242 us
  Pallas kernels  223 us (92%)
  local copies, waits for them, and re-layouts  7.48 us (3%)
  blocking collectives  5.79 us (2%)
  matrix products  3.89 us (2%)
    pallas_call x1, Pallas kernels, backprop(): pl.pallas_call(backprop_kernel, out_shape=(jax.ShapeDtypeStruct((3, token...  200 us
    pallas_call x1, Pallas kernels, sketch_sums(): pl.pallas_call(sketch_kernel, out_shape=jax.ShapeDtypeStruct((examples, 2...  23.2 us
    all_gather x1, blocking collectives, shards(): lax.all_gather(sketches.astype(jnp.bfloat16), 'dp', axis=0, tiled=True)  5.79 us

profile of v4, /device:TPU:0, one launch (start us, length us, event | category | flops | bytes accessed | tf_op | source)
XLA Modules:
  0.0 242.0 jit_solution(2276584547450257257)
XLA Ops:
  0.6 0.0 copy-start
  0.6 0.0 copy-start.1
  0.7 1.6 copy-done.1
  2.3 0.0 copy-start.2
  2.3 1.0 copy-done.2
  3.3 0.0 copy-start.3
  3.3 1.0 copy-done.3
  4.3 0.0 copy-start.4
  4.3 1.0 copy-done.4
  5.4 0.0 copy-start.5
  5.4 199.8 %shard_map.140 = (f32[3,448,64]{2,1,0:T(8,128)S(1)}, bf16[4,3696,2048]{2,1,0:T(8,128)(2,1)}) custom-call(bf16[3696,2048]{1,0:T(8,128)(2,1)} %w_ref.1, bf16[448,2048]{1,0:T(8,128)(2,1)S(1)} %copy-done.1, bf16[448,3696]{1,0:T(8,128)(2,1)} %gate_ref.1, bf16[448,3696]{1,0:T(8,128)(2,1)} %up_ref.1, bf16[64,3696]{1,0:T(8,128)(2,1)S(1)} %bitcast.28, ...), custom_call_target="tpu_custom_call" | custom-call | flops 27128758272 | bytes 121110528 | tf_op jit(solution)/shard_map/pallas_call | solution.py:370
  205.2 0.0 copy-start.6
  205.2 0.8 slice_bitcast_fusion
  206.0 0.0 copy-done
  206.0 0.0 copy-done.5
  206.0 0.0 copy-start.7
  206.0 0.6 fusion.15
  206.7 0.0 copy-done.6
  206.7 0.6 fusion.16
  207.3 0.0 copy-done.7
  207.3 0.0 copy-start.9
  207.3 0.6 fusion.17
  208.0 1.4 concatenate.3.proj_ref
  209.4 0.0 copy-start.8
  209.4 0.0 copy-done.9
  209.4 0.1 fusion.2
  209.5 0.1 copy.35.weight_ref
  209.6 23.2 %shard_map.141 = f32[2,2,64,128]{3,2,1,0:T(8,128)S(1)} custom-call(f32[448,384]{1,0:T(8,128)S(1)} %concatenate.3.proj_ref, f32[448,1]{1,0:T(8,128)S(1)} %copy.35.weight_ref), custom_call_target="tpu_custom_call" | custom-call | tf_op jit(solution)/shard_map/pallas_call | solution.py:489
  232.9 0.1 fusion.14
  233.0 0.1 multiply_reduce_fusion.1
  233.1 0.1 reshape.42
  233.2 0.7 fusion.13
  234.0 5.8 %all_gather.3 = bf16[8,3,4096]{2,1,0:T(4,128)(2,1)S(1)} all-gather(bf16[2,3,4096]{2,1,0:T(4,128)(2,1)S(1)} %copy.37), channel_id=1, replica_groups=mesh['parts'=2,'tensor'=4,'dp'=4] {'dp'}, dimensions={0}, use_global_device_ids=true | all-gather | bytes 245760 | tf_op jit(solution)/shard_map/all_gather | solution.py:564
  239.8 0.0 copy-done.8
  239.8 0.4 multiply_reduce_fusion
  240.3 0.1 reshape_reshape.3
  240.4 1.6 convolution_divide_fusion
  (4 shorter events, 0.1 us)
Async XLA Ops:
  0.6 205.4 %copy-start = (bf16[448,2048]{1,0:T(8,128)(2,1)S(1)}, bf16[448,2048]{1,0:T(8,128)(2,1)}, u32[]{:S(2)}) copy-start(bf16[448,2048]{1,0:T(8,128)(2,1)} %param.13) | copy-start | bytes 5505028
  0.6 1.6 copy-start.1
  2.3 1.0 copy-start.2
  3.3 1.0 copy-start.3
  4.3 1.0 copy-start.4
  5.4 200.7 %copy-start.5 = (bf16[2048,64]{0,1:T(8,128)(2,1)S(1)}, bf16[2048,64]{0,1:T(8,128)(2,1)}, u32[]{:S(2)}) copy-start(bf16[2048,64]{0,1:T(8,128)(2,1)} %param.18) | copy-start | bytes 786436
  205.2 1.5 copy-start.6
  206.0 1.3 copy-start.7
  207.3 2.1 copy-start.9
  209.4 30.4 %copy-start.8 = (s32[8]{0:T(128)S(1)}, s32[8]{0:T(128)}, u32[]{:S(2)}) copy-start(s32[8]{0:T(128)} %param.25) | copy-start | bytes 100
